TPU v7x, 32 devices: a whole 2x2x4 slice. The times are simulated.
32 devices in a mesh: grp: 4 (over z), dev: 8 (over y, x, core).
Axes of the slice: x: 2, y: 2, z: 4, core: 2. Of those that a mesh axis runs over, the one named last changes fastest.
Arguments:
- incident: bfloat16 [128, 128, 128], P(('grp', 'dev')), may hold values from -6 to 6
- tmatrix: bfloat16 [128, 128, 128], P(('grp', 'dev')), may hold values from -0.5 to 0.5
- blocks: bfloat16 [4096, 128, 128], P(('grp', 'dev')), may hold values from -0.09375 to 0.09375
- need: int32 [32, 8, 4], P(('grp', 'dev')), may hold values from 0 to 3, as said below
- pair_src: int32 [32, 512], P(('grp', 'dev')), may hold values from 0 to 31
- pair_tgt: int32 [32, 512], P(('grp', 'dev')), may hold values from 0 to 3
- pair_blk: int32 [32, 512], P(('grp', 'dev')), may hold values from 0 to 127
- pair_count: int32 [32], P(('grp', 'dev')), may hold values from 128 to 512, as said below
- factor: float32 [128, 2048], P(('grp', 'dev')), may hold values from -12 to 12
- harmonics: bfloat16 [2048, 128], replicated, may hold values from -0.046875 to 0.046875
- owner: int32 [2048], replicated, may hold values from 0 to 2047, each once
Outputs:
- amplitudes: float32 [2048, 128], P(('grp', 'dev'))
Inputs may be any that keep to these rules, and one draw needn't show every extreme that they name: Each row need[k, j] lists 4 distinct local spheres of peer j. `pair_count`: some device has exactly 512 live pairs.
All inputs are finite; a program needn't handle non-finite values.
Results may differ from a plain program's by a relative error of at most 0.0075.
Values may be sent and summed in bfloat16 or wider, within the bound.
A program may use at most 128 MiB of HBM per device.

v0:
```python
import jax
import jax.numpy as jnp
from jax import lax
from jax.sharding import PartitionSpec as P

SWEEPS = 2


def apply_tmatrix(tmatrix, field):
    return jnp.einsum("skl,slq->skq", tmatrix, field, preferred_element_type=jnp.float32).astype(
        jnp.bfloat16
    )


def scatter_pairs(sources, blocks, source_ids, target_ids, block_ids, live_count, spheres):
    pair_total = source_ids.shape[0]
    block_rows = pair_total // 4
    sphere_ids = jnp.arange(spheres, dtype=jnp.int32)

    def advance(running, offset):
        chosen_src = lax.dynamic_slice_in_dim(source_ids, offset, block_rows)
        chosen_tgt = lax.dynamic_slice_in_dim(target_ids, offset, block_rows)
        chosen_blk = lax.dynamic_slice_in_dim(block_ids, offset, block_rows)
        source_tiles = jnp.take(sources, chosen_src, axis=0)
        operators = jnp.take(blocks, chosen_blk, axis=0)
        contrib = jnp.einsum(
            "pkl,plq->pkq", operators, source_tiles, preferred_element_type=jnp.float32
        )
        pair_live = offset + jnp.arange(block_rows, dtype=jnp.int32) < live_count
        selector = ((chosen_tgt[None, :] == sphere_ids[:, None]) & pair_live[None, :]).astype(
            jnp.float32
        )
        added = jnp.einsum("sp,pkq->skq", selector, contrib, precision=lax.Precision.HIGHEST)
        return (running + added, None)

    start_rows = jnp.arange(4, dtype=jnp.int32) * block_rows
    initial = jnp.zeros((spheres, sources.shape[1], sources.shape[2]), jnp.float32)
    result, unused = lax.scan(advance, initial, start_rows)
    return result


def body(
    incident,
    tmatrix,
    blocks,
    need,
    pair_src,
    pair_tgt,
    pair_blk,
    pair_count,
    factor,
    harmonics,
    owner,
):
    spheres, coeff_rows, columns = incident.shape
    n_dev = lax.axis_size("dev")
    n_grp = lax.axis_size("grp")
    needed = need[0]
    incident_wide = incident.astype(jnp.float32)
    coeff = apply_tmatrix(tmatrix, incident)
    group_ids = (jnp.arange(n_dev, dtype=jnp.int32)[:, None] * spheres + needed).reshape(-1)
    source_ids = jnp.take(group_ids, pair_src[0])
    for sweep_index in range(SWEEPS):
        sources = lax.all_gather(coeff, "dev", axis=0, tiled=True)
        scattered = scatter_pairs(
            sources, blocks, source_ids, pair_tgt[0], pair_blk[0], pair_count[0], spheres
        )
        field = (incident_wide + scattered).astype(jnp.bfloat16)
        coeff = apply_tmatrix(tmatrix, field)
    rows_out = owner.shape[0] // (n_grp * n_dev)
    ordering = owner.reshape(n_grp, n_dev, rows_out).transpose(1, 0, 2).reshape(-1)
    table = jnp.take(harmonics, ordering, axis=0).astype(jnp.float32)
    phases = jnp.take(factor, ordering, axis=1)
    weighted = (phases[:, :, None] * table[None]).astype(jnp.bfloat16)
    amplitude = jnp.einsum("sdl,slq->dq", weighted, coeff, preferred_element_type=jnp.float32)
    partial_sum = lax.psum_scatter(amplitude, "dev", scatter_dimension=0, tiled=True)
    return lax.psum_scatter(partial_sum, "grp", scatter_dimension=0, tiled=True)


def solution(mesh):
    return jax.shard_map(
        body,
        mesh=mesh,
        in_specs=(
            P(("grp", "dev"), None, None),
            P(("grp", "dev"), None, None),
            P(("grp", "dev"), None, None),
            P(("grp", "dev"), None, None),
            P(("grp", "dev"), None),
            P(("grp", "dev"), None),
            P(("grp", "dev"), None),
            P(("grp", "dev")),
            P(("grp", "dev"), None),
            P(),
            P(),
        ),
        out_specs=P(("grp", "dev"), None),
        check_vma=False,
    )
```

profile of v0, /device:TPU:0, one launch (start us, length us, event | category | flops | bytes accessed | tf_op | source)
XLA Modules:
  0.0 395.8 jit_solution(6792211561784143419)
XLA Ops:
  18.1 16.5 %select_select_fusion = s32[512]{0:T(512)S(1)} fusion(pred[512]{0:T(512)(128)(4,1)S(1)} %get-tuple-element.210, pred[512]{0:T(512)(128)(4,1)S(1)} %get-tuple-element.209, pred[512]{0:T(512)(128)(4,1)S(1)} %get-tuple-element.208, pred[512]{0:T(512)(128)(4,1)S(1)} %get-tuple-element.207, pred[512]{0:T(512)(128)(4,1)S(1)} %get-tuple-element.206, ...), kind=kLoop, calls=%fused_computation.106 | loop fusion | flops 16384 | bytes 19044 | tf_op jit(solution)/shard_map/jit(_take)/select_n | solution.py:62
  35.5 134.7 %while.22 = (s32[]{:T(128)}, f32[4,128,128]{2,0,1:T(4,128)S(1)}, s32[4]{0:T(128)S(1)}, s32[512]{0:T(512)}, s32[]{:T(128)}, /*index=5*/s32[512]{0:T(512)}, bf16[1...) while((s32[]{:T(128)}, f32[4,128,128]{2,0,1:T(4,128)S(1)}, ...), condition=%wide.region_1.4_spmd.clone, body=%wide.region_0.3_spmd.clone.sunk | while | flops 641864448 | bytes 42482108 | solution.py:38
  48.5 8.0 %fusion.69 = f32[128,128,128]{2,1,0:T(8,128)} fusion(bf16[128,128,128]{2,1,0:T(8,128)(2,1)} %gather_fusion, bf16[128,128,128]{2,1,0:T(8,128)(2,1)} %gather_fusion.1, pred[128]{0:T(512)(128)(4,1)S(1)} %get-tuple-element.404, pred[128]{0:T(512)(128)(4,1)S(1)} %get-tuple-element.405), kind=kOutput, calls=%fused_computation.10.clone.1 | convolution fusion | flops 541065216 | bytes 16777472 | tf_op jit(solution)/shard_map/while/body/eval_jaxpr/pkl,plq->pkq/dot_general | solution.py:26
  58.7 10.5 %fusion.70 = f32[4,128,128]{2,0,1:T(4,128)S(1)} fusion(f32[128,128,128]{2,1,0:T(8,128)} %fusion.69, f32[4,128,128]{2,0,1:T(4,128)S(1)} %get-tuple-element.432, pred[]{:T(512)S(6)} %compare.131, s32[128]{0:T(128)S(1)} %dynamic_slice.46, pred[128]{0:T(512)(128)(4,1)S(1)} %add_compare_fusion.4), kind=kOutput, calls=%fused_computation.16.clone.1 | convolution fusion | flops 100795392 | bytes 8913537 | tf_op jit(solution)/shard_map/while/body/eval_jaxpr/sp,pkq->skq/dot_general | solution.py:33
  82.2 8.0 %fusion.69 = f32[128,128,128]{2,1,0:T(8,128)} fusion(bf16[128,128,128]{2,1,0:T(8,128)(2,1)} %gather_fusion, bf16[128,128,128]{2,1,0:T(8,128)(2,1)} %gather_fusion.1, pred[128]{0:T(512)(128)(4,1)S(1)} %get-tuple-element.404, pred[128]{0:T(512)(128)(4,1)S(1)} %get-tuple-element.405), kind=kOutput, calls=%fused_computation.10.clone.1 | convolution fusion | flops 541065216 | bytes 16777472 | tf_op jit(solution)/shard_map/while/body/eval_jaxpr/pkl,plq->pkq/dot_general | solution.py:26
  92.3 10.5 %fusion.70 = f32[4,128,128]{2,0,1:T(4,128)S(1)} fusion(f32[128,128,128]{2,1,0:T(8,128)} %fusion.69, f32[4,128,128]{2,0,1:T(4,128)S(1)} %get-tuple-element.432, pred[]{:T(512)S(6)} %compare.131, s32[128]{0:T(128)S(1)} %dynamic_slice.46, pred[128]{0:T(512)(128)(4,1)S(1)} %add_compare_fusion.4), kind=kOutput, calls=%fused_computation.16.clone.1 | convolution fusion | flops 100795392 | bytes 8913537 | tf_op jit(solution)/shard_map/while/body/eval_jaxpr/sp,pkq->skq/dot_general | solution.py:33
  115.9 8.0 %fusion.69 = f32[128,128,128]{2,1,0:T(8,128)} fusion(bf16[128,128,128]{2,1,0:T(8,128)(2,1)} %gather_fusion, bf16[128,128,128]{2,1,0:T(8,128)(2,1)} %gather_fusion.1, pred[128]{0:T(512)(128)(4,1)S(1)} %get-tuple-element.404, pred[128]{0:T(512)(128)(4,1)S(1)} %get-tuple-element.405), kind=kOutput, calls=%fused_computation.10.clone.1 | convolution fusion | flops 541065216 | bytes 16777472 | tf_op jit(solution)/shard_map/while/body/eval_jaxpr/pkl,plq->pkq/dot_general | solution.py:26
  126.0 10.5 %fusion.70 = f32[4,128,128]{2,0,1:T(4,128)S(1)} fusion(f32[128,128,128]{2,1,0:T(8,128)} %fusion.69, f32[4,128,128]{2,0,1:T(4,128)S(1)} %get-tuple-element.432, pred[]{:T(512)S(6)} %compare.131, s32[128]{0:T(128)S(1)} %dynamic_slice.46, pred[128]{0:T(512)(128)(4,1)S(1)} %add_compare_fusion.4), kind=kOutput, calls=%fused_computation.16.clone.1 | convolution fusion | flops 100795392 | bytes 8913537 | tf_op jit(solution)/shard_map/while/body/eval_jaxpr/sp,pkq->skq/dot_general | solution.py:33
  149.6 8.0 %fusion.69 = f32[128,128,128]{2,1,0:T(8,128)} fusion(bf16[128,128,128]{2,1,0:T(8,128)(2,1)} %gather_fusion, bf16[128,128,128]{2,1,0:T(8,128)(2,1)} %gather_fusion.1, pred[128]{0:T(512)(128)(4,1)S(1)} %get-tuple-element.404, pred[128]{0:T(512)(128)(4,1)S(1)} %get-tuple-element.405), kind=kOutput, calls=%fused_computation.10.clone.1 | convolution fusion | flops 541065216 | bytes 16777472 | tf_op jit(solution)/shard_map/while/body/eval_jaxpr/pkl,plq->pkq/dot_general | solution.py:26
  159.7 10.5 %fusion.70 = f32[4,128,128]{2,0,1:T(4,128)S(1)} fusion(f32[128,128,128]{2,1,0:T(8,128)} %fusion.69, f32[4,128,128]{2,0,1:T(4,128)S(1)} %get-tuple-element.432, pred[]{:T(512)S(6)} %compare.131, s32[128]{0:T(128)S(1)} %dynamic_slice.46, pred[128]{0:T(512)(128)(4,1)S(1)} %add_compare_fusion.4), kind=kOutput, calls=%fused_computation.16.clone.1 | convolution fusion | flops 100795392 | bytes 8913537 | tf_op jit(solution)/shard_map/while/body/eval_jaxpr/sp,pkq->skq/dot_general | solution.py:33
  171.7 5.5 %gather_fusion.4 = f32[2048,4]{1,0:T(8,128)S(1)} fusion(f32[4,2048]{0,1:T(8,128)S(1)} %copy.36, s32[2048]{0:T(1024)S(1)} %broadcast_clamp_fusion), kind=kCustom, calls=%fused_computation.4 | custom fusion | bytes 73728 | tf_op jit(solution)/shard_map/jit(_take)/gather | solution.py:73
  177.8 6.2 %gather_fusion.5 = bf16[2048,128]{1,0:T(8,128)(2,1)S(1)} fusion(bf16[2048,128]{1,0:T(8,128)(2,1)S(1)} %copy-done, s32[2048]{0:T(1024)S(1)} %broadcast_clamp_fusion), kind=kCustom, calls=%fused_computation.5 | custom fusion | bytes 1056768 | tf_op jit(solution)/shard_map/jit(_take)/gather | solution.py:72
  184.4 12.5 %all-gather.5.cloned.1.call-done = bf16[32,128,128]{2,1,0:T(8,128)(2,1)} async-done(((bf16[4,128,128]{2,1,0:T(8,128)(2,1)}), bf16[32,128,128]{2,1,0:T(8,128)(2,1)}) %all-gather.5.cloned.1.call-update) | async-done | bytes 1048592 | tf_op jit(solution)/shard_map/all_gather | solution.py:64
  196.9 132.4 %while.23 = (s32[]{:T(128)}, f32[4,128,128]{2,0,1:T(4,128)S(1)}, s32[4]{0:T(128)S(1)}, s32[512]{0:T(512)}, s32[]{:T(128)}, /*index=5*/s32[512]{0:T(512)}, bf16[1...) while((s32[]{:T(128)}, f32[4,128,128]{2,0,1:T(4,128)S(1)}, ...), condition=%wide.region_3.6_spmd.clone, body=%wide.region_2.5_spmd.clone.sunk | while | flops 641864448 | bytes 42482108 | solution.py:38
  209.5 8.0 %fusion.75 = f32[128,128,128]{2,1,0:T(8,128)} fusion(bf16[128,128,128]{2,1,0:T(8,128)(2,1)} %gather_fusion.2, bf16[128,128,128]{2,1,0:T(8,128)(2,1)} %gather_fusion.3, pred[128]{0:T(512)(128)(4,1)S(1)} %get-tuple-element.417, pred[128]{0:T(512)(128)(4,1)S(1)} %get-tuple-element.418), kind=kOutput, calls=%fused_computation.32.clone.1 | convolution fusion | flops 541065216 | bytes 16777472 | tf_op jit(solution)/shard_map/while/body/eval_jaxpr/pkl,plq->pkq/dot_general | solution.py:26
  219.5 10.5 %fusion.76 = f32[4,128,128]{2,0,1:T(4,128)S(1)} fusion(f32[128,128,128]{2,1,0:T(8,128)} %fusion.75, f32[4,128,128]{2,0,1:T(4,128)S(1)} %get-tuple-element.468, pred[]{:T(512)S(6)} %compare.132, s32[128]{0:T(128)S(1)} %dynamic_slice.48, pred[128]{0:T(512)(128)(4,1)S(1)} %add_compare_fusion.5), kind=kOutput, calls=%fused_computation.38.clone.1 | convolution fusion | flops 100795392 | bytes 8913537 | tf_op jit(solution)/shard_map/while/body/eval_jaxpr/sp,pkq->skq/dot_general | solution.py:33
  242.6 8.0 %fusion.75 = f32[128,128,128]{2,1,0:T(8,128)} fusion(bf16[128,128,128]{2,1,0:T(8,128)(2,1)} %gather_fusion.2, bf16[128,128,128]{2,1,0:T(8,128)(2,1)} %gather_fusion.3, pred[128]{0:T(512)(128)(4,1)S(1)} %get-tuple-element.417, pred[128]{0:T(512)(128)(4,1)S(1)} %get-tuple-element.418), kind=kOutput, calls=%fused_computation.32.clone.1 | convolution fusion | flops 541065216 | bytes 16777472 | tf_op jit(solution)/shard_map/while/body/eval_jaxpr/pkl,plq->pkq/dot_general | solution.py:26
  252.6 10.5 %fusion.76 = f32[4,128,128]{2,0,1:T(4,128)S(1)} fusion(f32[128,128,128]{2,1,0:T(8,128)} %fusion.75, f32[4,128,128]{2,0,1:T(4,128)S(1)} %get-tuple-element.468, pred[]{:T(512)S(6)} %compare.132, s32[128]{0:T(128)S(1)} %dynamic_slice.48, pred[128]{0:T(512)(128)(4,1)S(1)} %add_compare_fusion.5), kind=kOutput, calls=%fused_computation.38.clone.1 | convolution fusion | flops 100795392 | bytes 8913537 | tf_op jit(solution)/shard_map/while/body/eval_jaxpr/sp,pkq->skq/dot_general | solution.py:33
  275.7 8.0 %fusion.75 = f32[128,128,128]{2,1,0:T(8,128)} fusion(bf16[128,128,128]{2,1,0:T(8,128)(2,1)} %gather_fusion.2, bf16[128,128,128]{2,1,0:T(8,128)(2,1)} %gather_fusion.3, pred[128]{0:T(512)(128)(4,1)S(1)} %get-tuple-element.417, pred[128]{0:T(512)(128)(4,1)S(1)} %get-tuple-element.418), kind=kOutput, calls=%fused_computation.32.clone.1 | convolution fusion | flops 541065216 | bytes 16777472 | tf_op jit(solution)/shard_map/while/body/eval_jaxpr/pkl,plq->pkq/dot_general | solution.py:26
  285.7 10.5 %fusion.76 = f32[4,128,128]{2,0,1:T(4,128)S(1)} fusion(f32[128,128,128]{2,1,0:T(8,128)} %fusion.75, f32[4,128,128]{2,0,1:T(4,128)S(1)} %get-tuple-element.468, pred[]{:T(512)S(6)} %compare.132, s32[128]{0:T(128)S(1)} %dynamic_slice.48, pred[128]{0:T(512)(128)(4,1)S(1)} %add_compare_fusion.5), kind=kOutput, calls=%fused_computation.38.clone.1 | convolution fusion | flops 100795392 | bytes 8913537 | tf_op jit(solution)/shard_map/while/body/eval_jaxpr/sp,pkq->skq/dot_general | solution.py:33
  308.8 8.0 %fusion.75 = f32[128,128,128]{2,1,0:T(8,128)} fusion(bf16[128,128,128]{2,1,0:T(8,128)(2,1)} %gather_fusion.2, bf16[128,128,128]{2,1,0:T(8,128)(2,1)} %gather_fusion.3, pred[128]{0:T(512)(128)(4,1)S(1)} %get-tuple-element.417, pred[128]{0:T(512)(128)(4,1)S(1)} %get-tuple-element.418), kind=kOutput, calls=%fused_computation.32.clone.1 | convolution fusion | flops 541065216 | bytes 16777472 | tf_op jit(solution)/shard_map/while/body/eval_jaxpr/pkl,plq->pkq/dot_general | solution.py:26
  318.8 10.5 %fusion.76 = f32[4,128,128]{2,0,1:T(4,128)S(1)} fusion(f32[128,128,128]{2,1,0:T(8,128)} %fusion.75, f32[4,128,128]{2,0,1:T(4,128)S(1)} %get-tuple-element.468, pred[]{:T(512)S(6)} %compare.132, s32[128]{0:T(128)S(1)} %dynamic_slice.48, pred[128]{0:T(512)(128)(4,1)S(1)} %add_compare_fusion.5), kind=kOutput, calls=%fused_computation.38.clone.1 | convolution fusion | flops 100795392 | bytes 8913537 | tf_op jit(solution)/shard_map/while/body/eval_jaxpr/sp,pkq->skq/dot_general | solution.py:33
  331.8 36.1 %reduce-scatter.3.cloned.1.call-done = f32[256,128]{1,0:T(8,128)} async-done(((f32[2048,128]{1,0:T(8,128)}), f32[256,128]{1,0:T(8,128)}) %reduce-scatter.3.cloned.1.call-update) | async-done | bytes 131088 | tf_op jit(solution)/shard_map/reduce_scatter | solution.py:76
  368.0 21.3 %reduce-scatter.5.cloned.1.call-done = f32[64,128]{1,0:T(8,128)} async-done(((f32[256,128]{1,0:T(8,128)}), f32[64,128]{1,0:T(8,128)}) %reduce-scatter.5.cloned.1.call-update) | async-done | bytes 32784 | tf_op jit(solution)/shard_map/reduce_scatter | solution.py:77
  (109 shorter events, 120.8 us)
Async XLA Ops:
  6.5 171.3 %copy-start = (bf16[2048,128]{1,0:T(8,128)(2,1)S(1)}, bf16[2048,128]{1,0:T(8,128)(2,1)}, u32[]{:S(2)}) copy-start(bf16[2048,128]{1,0:T(8,128)(2,1)} %param.28) | copy-start | bytes 1572868
  6.5 28.9 %all-gather.3.cloned.1.call-start = ((), (), s32[]{:S(2)}) async-start(), calls=%async_computation.2 | async-start | bytes 1179648 | tf_op jit(solution)/shard_map/all_gather | solution.py:64
  8.4 188.5 %all-gather.5.cloned.1.call-start = ((), (), s32[]{:S(2)}) async-start(), calls=%async_computation.3 | async-start | bytes 1179648 | tf_op jit(solution)/shard_map/all_gather | solution.py:64
  35.5 134.7 %copy-start.1 = (bf16[4,128,128]{2,1,0:T(8,128)(2,1)S(1)}, bf16[4,128,128]{2,1,0:T(8,128)(2,1)}, u32[]{:S(2)}) copy-start(bf16[4,128,128]{2,1,0:T(8,128)(2,1)} %param.19) | copy-start | bytes 393220
  35.5 134.9 %copy-start.2 = (bf16[4,128,128]{2,1,0:T(8,128)(2,1)S(1)}, bf16[4,128,128]{2,1,0:T(8,128)(2,1)}, u32[]{:S(2)}) copy-start(bf16[4,128,128]{2,1,0:T(8,128)(2,1)} %param.20) | copy-start | bytes 393220
  171.4 196.6 %reduce-scatter.3.cloned.1.call-start = ((), (), s32[]{:S(2)}) async-start(), calls=%async_computation.4 | async-start | bytes 1179648 | tf_op jit(solution)/shard_map/reduce_scatter | solution.py:76
  331.8 57.5 %reduce-scatter.5.cloned.1.call-start = ((), (), s32[]{:S(2)}) async-start(), calls=%async_computation.5 | async-start | bytes 163840 | tf_op jit(solution)/shard_map/reduce_scatter | solution.py:77
Sparse Core Ops, SparseCore 0:
  9.2 26.1 all-gather.2
  171.5 25.3 all-gather.4
  331.9 36.0 reduce-scatter.2
  370.1 19.1 reduce-scatter.4
where the time goes:
time: 398 us; the launch traced here: 396 us
  matrix products  153 us (38%)
  local copies, waits for them, and re-layouts  104 us (26%)
  waiting for transfers between devices  70.9 us (18%)
  other arithmetic  39 us (10%)
  loops' own time  15.3 us (4%)
  between operations  13.3 us (3%)
    dot_general x8, matrix products, advance(): jnp.einsum('sp,pkq->skq', selector, contrib, precision=lax.Precision.HIGH...  84 us
    dot_general x8, matrix products, advance(): jnp.einsum('pkl,plq->pkq', operators, source_tiles, preferred_element_typ...  64.3 us
    gather x8, local copies, waits for them, and re-layouts, advance(): operators = jnp.take(blocks, chosen_blk, axis=0)  41.8 us
    reduce_scatter x1, waiting for transfers between devices, body(): lax.psum_scatter(amplitude, 'dev', scatter_dimension=0, tiled=True)  36.1 us
    gather x8, local copies, waits for them, and re-layouts, advance(): source_tiles = jnp.take(sources, chosen_src, axis=0)  34.3 us
    reduce_scatter x1, waiting for transfers between devices, body(): return lax.psum_scatter(partial_sum, 'grp', scatter_dimension=0, tiled=True)  21.3 us
    select_n x1, other arithmetic, body(): source_ids = jnp.take(group_ids, pair_src[0])  16.5 us
    another operation x2, loops' own time, scatter_pairs(): result, unused = lax.scan(advance, initial, start_rows)  15.3 us
  transfers between devices with their start and end apart: 4, of which 4 were waited for; matrix products, arithmetic and copies ran while one was open for 10% of the time, Pallas kernels for 0%

commit v1 on v0

v1 whole, which is shorter than its diff:
```python
import functools

import jax
import jax.numpy as jnp
from jax import lax
from jax.experimental import pallas as pl
from jax.experimental.pallas import tpu as pltpu
from jax.sharding import PartitionSpec as P

SWEEPS = 2
MESH = pl.DeviceIdType.MESH


def bits_for(size):
    return max(1, (size - 1).bit_length())


def flipped(index, mask):
    result = index
    bit = 1
    while bit <= mask:
        if mask & bit:
            result = result + bit * (1 - 2 * ((index // bit) % 2))
        bit *= 2
    return result


def kernel(
    n_grp,
    n_dev,
    count_ref,
    need_ref,
    owner_ref,
    src_ref,
    tgt_ref,
    blk_ref,
    incident_ref,
    tmatrix_ref,
    factor_ref,
    blocks_hbm,
    harmonics_hbm,
    out_ref,
    blocks,
    harmonics,
    sums,
    operator,
    coeffs,
    final,
    table,
    gathered,
    weighted,
    scattered,
    part_send,
    part_recv,
    group_sum,
    z_send,
    z_recv,
    value_col,
    rank_col,
    factor_pad,
    meta,
    meta_smem,
    load_sem,
    send_sem,
    recv_sem,
    z_send_sem,
    z_recv_sem,
):
    grp = lax.axis_index("grp")
    dev = lax.axis_index("dev")
    spheres, rows, cols = incident_ref.shape
    n_blk = blocks.shape[0]
    pairs = src_ref.shape[1]
    slots = n_dev * spheres
    cells = spheres * slots
    n_dir = harmonics.shape[0]
    rows_out = out_ref.shape[0]
    f32 = jnp.float32
    lanes = 128

    barrier = pltpu.get_barrier_semaphore()
    for m in range(1, n_dev):
        pl.semaphore_signal(barrier, inc=1, device_id=(grp, flipped(dev, m)), device_id_type=MESH)
    for m in range(1, n_grp):
        pl.semaphore_signal(barrier, inc=1, device_id=((grp + m) % n_grp, dev), device_id_type=MESH)
    load_blocks = pltpu.make_async_copy(blocks_hbm, blocks, load_sem.at[0])
    load_blocks.start()
    load_harmonics = pltpu.make_async_copy(harmonics_hbm, harmonics, load_sem.at[1])
    load_harmonics.start()

    def gather_copy(sweep, source, target):
        return pltpu.make_async_remote_copy(
            src_ref=coeffs.at[sweep, source],
            dst_ref=coeffs.at[sweep, source],
            send_sem=send_sem.at[sweep, target],
            recv_sem=recv_sem.at[sweep, source],
            device_id=(grp, target),
            device_id_type=MESH,
        )

    def send_coeffs(sweep):
        for m in range(1, n_dev):
            gather_copy(sweep, dev, flipped(dev, m)).start()

    def apply_tmatrix(s, field):
        return jnp.dot(tmatrix_ref[s], field, preferred_element_type=f32).astype(jnp.bfloat16)

    for s in range(spheres):
        coeffs[0, dev, s * rows : (s + 1) * rows, :] = apply_tmatrix(s, incident_ref[s])
    pl.semaphore_wait(barrier, n_dev - 1 + n_grp - 1)
    send_coeffs(0)

    blk_bits, pair_bits = bits_for(n_blk), bits_for(pairs)
    place = lax.broadcasted_iota(jnp.int32, (1, pairs), 1)
    key = jnp.where(place < count_ref[0], tgt_ref[...] * slots + src_ref[...], cells)
    value = (((key << pair_bits) + place) << blk_bits) + blk_ref[...]
    value_col[...] = jnp.transpose(jnp.broadcast_to(value, (lanes, pairs)))
    col = value_col[...]

    def count(hits):
        return jnp.sum(jnp.where(hits, 1, 0), axis=0, keepdims=True)

    rank = jnp.concatenate(
        [count(col < value[:, k : k + lanes]) for k in range(0, pairs, lanes)], axis=1
    )
    rank_col[...] = jnp.transpose(jnp.broadcast_to(rank, (lanes, pairs)))
    key_col = col >> (blk_bits + pair_bits)
    for k in range(0, pairs, lanes):
        spot = lax.broadcasted_iota(jnp.int32, (1, lanes), 1) + k
        hit = rank_col[...] == spot
        ordered = jnp.sum(jnp.where(hit, col, 0), axis=0, keepdims=True)
        meta[0:1, k : k + lanes] = ordered & ((1 << blk_bits) - 1)
        meta[1:2, k : k + lanes] = ordered >> (blk_bits + pair_bits)
    for k in range(0, cells, lanes):
        spot = lax.broadcasted_iota(jnp.int32, (1, lanes), 1) + k
        upto, under = count(key_col <= spot), count(key_col < spot)
        meta[2:3, k : k + lanes] = jnp.where(upto > under, upto - 1, pairs)
    to_smem = pltpu.make_async_copy(meta, meta_smem, load_sem.at[2])
    to_smem.start()
    to_smem.wait()
    load_blocks.wait()

    sums[pairs] = jnp.zeros((rows, rows), jnp.bfloat16)
    step = 4

    def add_blocks(i, total):
        for k in range(step):
            at = i * step + k
            before = jnp.maximum(at - 1, 0)
            keep = jnp.where(meta_smem[1, at] == meta_smem[1, before], 1.0, 0.0)
            block = jnp.clip(meta_smem[0, at], 0, n_blk - 1)
            total = total * keep + blocks[block].astype(f32)
            sums[at] = total.astype(jnp.bfloat16)
        return total

    lax.fori_loop(0, pairs // step, add_blocks, jnp.zeros((rows, rows), f32))

    def place_cells(j, carry):
        for u in range(spheres):
            slot = 0
            for c in range(1, spheres):
                slot = slot + jnp.where(need_ref[0, j, c] == u, c, 0)
            slot = jnp.minimum(slot, spheres - 1)
            for t in range(spheres):
                last = meta_smem[2, t * slots + j * spheres + slot]
                total = sums[jnp.clip(last, 0, pairs)]
                operator[j, t * rows : (t + 1) * rows, u * rows : (u + 1) * rows] = total
        return carry

    lax.fori_loop(0, n_dev, place_cells, 0)

    def sweep_sum(sweep):
        scattered[...] = jnp.dot(operator[dev], coeffs[sweep, dev], preferred_element_type=f32)
        for m in range(1, n_dev):
            peer = flipped(dev, m)
            gather_copy(sweep, peer, dev).wait_recv()
            scattered[...] += jnp.dot(operator[peer], coeffs[sweep, peer], preferred_element_type=f32)

    def field_of(s):
        wide = incident_ref[s].astype(f32) + scattered[s * rows : (s + 1) * rows, :]
        return wide.astype(jnp.bfloat16)

    sweep_sum(0)
    for s in range(spheres):
        coeffs[1, dev, s * rows : (s + 1) * rows, :] = apply_tmatrix(s, field_of(s))
    send_coeffs(1)

    load_harmonics.wait()
    factor_pad[...] = jnp.zeros_like(factor_pad)
    for k in range(0, n_dir, lanes):
        factor_pad[0:spheres, :] = factor_ref[:, k : k + lanes]
        table[k : k + lanes, lanes:] = jnp.transpose(factor_pad[...])
        table[k : k + lanes, :lanes] = harmonics[k : k + lanes, :].astype(f32)
    chunk = n_grp * rows_out
    row_step = 8

    def weigh(p, carry):
        for z in range(n_grp):

            def fetch(i, inner):
                for k in range(row_step):
                    row = i * row_step + k
                    source = owner_ref[(z * n_dev + p) * rows_out + row]
                    gathered[pl.ds(z * rows_out + row, 1), :] = table[pl.ds(source, 1), :]
                return inner

            lax.fori_loop(0, rows_out // row_step, fetch, 0)
        for s in range(spheres):
            phase = gathered[:, lanes + s : lanes + s + 1]
            product = phase * gathered[:, :lanes]
            weighted[p, :, s * lanes : (s + 1) * lanes] = product.astype(jnp.bfloat16)
        return carry

    lax.fori_loop(0, n_dev, weigh, 0)

    sweep_sum(1)
    for s in range(spheres):
        final[s * rows : (s + 1) * rows, :] = apply_tmatrix(s, field_of(s))

    def part_copy(source, target):
        return pltpu.make_async_remote_copy(
            src_ref=part_send.at[target],
            dst_ref=part_recv.at[source],
            send_sem=send_sem.at[SWEEPS, target],
            recv_sem=recv_sem.at[SWEEPS, source],
            device_id=(grp, target),
            device_id_type=MESH,
        )

    for m in range(1, n_dev):
        peer = flipped(dev, m)
        part = jnp.dot(weighted[peer], final[...], preferred_element_type=f32)
        part_send[peer] = part.astype(part_send.dtype)
        part_copy(dev, peer).start()
    group_sum[...] = jnp.dot(weighted[dev], final[...], preferred_element_type=f32)
    for m in range(1, n_dev):
        peer = flipped(dev, m)
        part_copy(peer, dev).wait_recv()
        group_sum[...] += part_recv[peer].astype(f32)

    def z_copy(source, target):
        return pltpu.make_async_remote_copy(
            src_ref=z_send.at[target],
            dst_ref=z_recv.at[source],
            send_sem=z_send_sem.at[target],
            recv_sem=z_recv_sem.at[source],
            device_id=(target, dev),
            device_id_type=MESH,
        )

    for z in range(n_grp):
        z_send[z] = group_sum[z * rows_out : (z + 1) * rows_out, :].astype(z_send.dtype)
    for m in range(1, n_grp):
        z_copy(grp, (grp + m) % n_grp).start()
    start = pl.multiple_of(grp * rows_out, rows_out)
    out_ref[...] = group_sum[pl.ds(start, rows_out), :]
    for m in range(1, n_grp):
        peer = (grp + m) % n_grp
        z_copy(peer, grp).wait_recv()
        out_ref[...] += z_recv[peer].astype(f32)
    for m in range(1, n_grp):
        z_copy(grp, (grp + m) % n_grp).wait_send()
    for m in range(1, n_dev):
        peer = flipped(dev, m)
        for sweep in range(SWEEPS):
            gather_copy(sweep, dev, peer).wait_send()
        part_copy(dev, peer).wait_send()


def body(
    incident,
    tmatrix,
    blocks,
    need,
    pair_src,
    pair_tgt,
    pair_blk,
    pair_count,
    factor,
    harmonics,
    owner,
):
    n_dev = lax.axis_size("dev")
    n_grp = lax.axis_size("grp")
    spheres, rows, cols = incident.shape
    n_blk = blocks.shape[0]
    pairs = pair_src.shape[1]
    n_dir = harmonics.shape[0]
    rows_out = n_dir // (n_grp * n_dev)
    chunk = n_grp * rows_out
    wide = spheres * rows
    bf16, f32 = jnp.bfloat16, jnp.float32
    z_type = bf16 if rows_out % 16 == 0 else f32
    meta_shape = (8, max(pairs, spheres * n_dev * spheres))
    smem = pl.BlockSpec(memory_space=pltpu.SMEM)
    vmem = pl.BlockSpec(memory_space=pltpu.VMEM)
    anywhere = pl.BlockSpec(memory_space=pl.ANY)
    dma = pltpu.SemaphoreType.DMA
    return pl.pallas_call(
        functools.partial(kernel, n_grp, n_dev),
        out_shape=jax.ShapeDtypeStruct((rows_out, cols), f32),
        in_specs=[smem] * 3 + [vmem] * 6 + [anywhere] * 2,
        out_specs=vmem,
        scratch_shapes=[
            pltpu.VMEM(blocks.shape, bf16),
            pltpu.VMEM(harmonics.shape, bf16),
            pltpu.VMEM((pairs + 1, rows, rows), bf16),
            pltpu.VMEM((n_dev, wide, wide), bf16),
            pltpu.VMEM((SWEEPS, n_dev, wide, cols), bf16),
            pltpu.VMEM((wide, cols), bf16),
            pltpu.VMEM((n_dir, 256), f32),
            pltpu.VMEM((chunk, 256), f32),
            pltpu.VMEM((n_dev, chunk, wide), bf16),
            pltpu.VMEM((wide, cols), f32),
            pltpu.VMEM((n_dev, chunk, cols), bf16),
            pltpu.VMEM((n_dev, chunk, cols), bf16),
            pltpu.VMEM((chunk, cols), f32),
            pltpu.VMEM((n_grp, rows_out, cols), z_type),
            pltpu.VMEM((n_grp, rows_out, cols), z_type),
            pltpu.VMEM((pairs, 128), jnp.int32),
            pltpu.VMEM((pairs, 128), jnp.int32),
            pltpu.VMEM((128, 128), f32),
            pltpu.VMEM(meta_shape, jnp.int32),
            pltpu.SMEM(meta_shape, jnp.int32),
            dma((3,)),
            dma((SWEEPS + 1, n_dev)),
            dma((SWEEPS + 1, n_dev)),
            dma((n_grp,)),
            dma((n_grp,)),
        ],
        compiler_params=pltpu.CompilerParams(
            collective_id=0, has_side_effects=True, vmem_limit_bytes=60 * 1024 * 1024
        ),
    )(
        pair_count,
        need,
        owner,
        pair_src,
        pair_tgt,
        pair_blk,
        incident,
        tmatrix,
        factor,
        blocks,
        harmonics,
    )


def solution(mesh):
    return jax.shard_map(
        body,
        mesh=mesh,
        in_specs=(
            P(("grp", "dev"), None, None),
            P(("grp", "dev"), None, None),
            P(("grp", "dev"), None, None),
            P(("grp", "dev"), None, None),
            P(("grp", "dev"), None),
            P(("grp", "dev"), None),
            P(("grp", "dev"), None),
            P(("grp", "dev")),
            P(("grp", "dev"), None),
            P(),
            P(),
        ),
        out_specs=P(("grp", "dev"), None),
        check_vma=False,
    )
```

time: 398 us -> 50.4 us (0.13)
  matrix products: 153 us -> 0 us
  local copies, waits for them, and re-layouts: 104 us -> 2.72 us
  waiting for transfers between devices: 70.9 us -> 0 us
  Pallas kernels: 0 us -> 46.8 us
  other arithmetic: 39 us -> 0 us
  loops' own time: 15.3 us -> 0 us
  between operations: 13.3 us -> 0.66 us
    dot_general x19 -> x0, matrix products: 153 us -> none  [the longest x8 84 us: advance(): jnp.einsum('sp,pkq->skq', selector, contrib, precision=lax.Precision.HIGH...]
    gather x20 -> x0, local copies, waits for them, and re-layouts: 89.2 us -> none  [the longest x8 41.8 us: advance(): operators = jnp.take(blocks, chosen_blk, axis=0)]
    reduce_scatter x2 -> x0, waiting for transfers between devices: 57.4 us -> none  [the longest x1 36.1 us: body(): lax.psum_scatter(amplitude, 'dev', scatter_dimension=0, tiled=True)]
    pallas_call x0 -> x1, Pallas kernels: none -> 46.8 us  [body(): pl.pallas_call(functools.partial(kernel, n_grp, n_dev), out_shape=jax.Sha...]
    select_n x3 -> x0, other arithmetic: 16.8 us -> none  [the longest x1 16.5 us: body(): source_ids = jnp.take(group_ids, pair_src[0])]
    another operation x2 -> x0, loops' own time: 15.3 us -> none  [scatter_pairs(): result, unused = lax.scan(advance, initial, start_rows)]
    all_gather x2 -> x0, waiting for transfers between devices: 13.4 us -> none  [body(): sources = lax.all_gather(coeff, 'dev', axis=0, tiled=True)]
    dynamic_slice x16 -> x0, local copies, waits for them, and re-layouts: 11 us -> none  [the longest x8 6.03 us: advance(): chosen_tgt = lax.dynamic_slice_in_dim(target_ids, offset, block_rows)]
  transfers between devices with their start and end apart: 4 -> 0, of which waited for: 4 -> 0; matrix products, arithmetic and copies ran while one was open for 10% -> 0% of each run, Pallas kernels for 0% -> 0%
where the time goes in v1:
time: 50.4 us; the launch traced here: 50.1 us
  Pallas kernels  46.8 us (93%)
  local copies, waits for them, and re-layouts  2.72 us (5%)
  between operations  0.66 us (1%)
    pallas_call x1, Pallas kernels, body(): pl.pallas_call(functools.partial(kernel, n_grp, n_dev), out_shape=jax.Sha...  46.8 us
    unnamed x2, local copies, waits for them, and re-layouts  2.72 us

profile of v1, /device:TPU:0, one launch (start us, length us, event | category | flops | bytes accessed | tf_op | source)
XLA Modules:
  0.0 50.1 jit_solution(15360297472000319776)
XLA Ops:
  0.7 1.3 %copy.12.need_ref = s32[1,8,4]{2,1,0:T(8,128)} copy(s32[1,8,4]{1,2,0:T(4,128)} %param.14) | data formatting | bytes 256 | tf_op args[3]
  2.0 46.8 %shard_map.109 = f32[64,128]{1,0:T(8,128)} custom-call(s32[1]{0:T(128)S(6)} %copy.14.count_ref, s32[1,8,4]{2,1,0:T(8,128)} %copy.12.need_ref, s32[2048]{0:T(1024)} %owner_ref.1, s32[1,512]{1,0:T(1,128)} %src_ref.1, s32[1,512]{1,0:T(1,128)} %tgt_ref.1, s32[1,512]{1,0:T(1,128)} %blk_ref.1, bf16[4,128,128]{2,1,0:T(8,128)(2,1)} %incident_ref.1, ...), custom_call_target="tpu_custom_call" | custom-call | tf_op jit(solution)/shard_map/pallas_call | solution.py:299
  48.8 1.4 %copy.15 = f32[64,128]{1,0:T(8,128)} copy(f32[64,128]{1,0:T(8,128)} %shard_map.109) | data formatting | bytes 65536

commit v2 on v1

--- a/solution.py
+++ b/solution.py
@@ -29,8 +29,8 @@
     n_grp,
     n_dev,
     count_ref,
+    owner_ref,
     need_ref,
-    owner_ref,
     src_ref,
     tgt_ref,
     blk_ref,
@@ -52,6 +52,8 @@
     scattered,
     part_send,
     part_recv,
+    pair_send,
+    pair_recv,
     group_sum,
     z_send,
     z_recv,
@@ -88,19 +90,36 @@
     load_harmonics = pltpu.make_async_copy(harmonics_hbm, harmonics, load_sem.at[1])
     load_harmonics.start()
 
-    def gather_copy(sweep, source, target):
+    def gather_copy(sweep, source, target, mask):
         return pltpu.make_async_remote_copy(
             src_ref=coeffs.at[sweep, source],
             dst_ref=coeffs.at[sweep, source],
-            send_sem=send_sem.at[sweep, target],
+            send_sem=send_sem.at[sweep, mask],
             recv_sem=recv_sem.at[sweep, source],
             device_id=(grp, target),
             device_id_type=MESH,
         )
 
+    sibling = flipped(dev, 1)
+    others = list(range(2, n_dev, 2))
+
+    def own_copy(sweep, mask):
+        return gather_copy(sweep, dev, flipped(dev, mask), mask)
+
+    def relay_copy(sweep, mask):
+        return gather_copy(sweep, flipped(dev, mask), sibling, mask + 1)
+
+    def arrival(sweep, mask):
+        return gather_copy(sweep, flipped(dev, mask), dev, mask)
+
     def send_coeffs(sweep):
-        for m in range(1, n_dev):
-            gather_copy(sweep, dev, flipped(dev, m)).start()
+        for m in others[::-1] + [1]:
+            own_copy(sweep, m).start()
+
+    def relay(sweep):
+        for m in others:
+            arrival(sweep, m).wait_recv()
+            relay_copy(sweep, m).start()
 
     def apply_tmatrix(s, field):
         return jnp.dot(tmatrix_ref[s], field, preferred_element_type=f32).astype(jnp.bfloat16)
@@ -135,6 +154,7 @@
         spot = lax.broadcasted_iota(jnp.int32, (1, lanes), 1) + k
         upto, under = count(key_col <= spot), count(key_col < spot)
         meta[2:3, k : k + lanes] = jnp.where(upto > under, upto - 1, pairs)
+    meta[8 : 8 + n_dev, 0:spheres] = need_ref[0]
     to_smem = pltpu.make_async_copy(meta, meta_smem, load_sem.at[2])
     to_smem.start()
     to_smem.wait()
@@ -155,11 +175,13 @@
 
     lax.fori_loop(0, pairs // step, add_blocks, jnp.zeros((rows, rows), f32))
 
+    relay(0)
+
     def place_cells(j, carry):
         for u in range(spheres):
             slot = 0
             for c in range(1, spheres):
-                slot = slot + jnp.where(need_ref[0, j, c] == u, c, 0)
+                slot = slot + jnp.where(meta_smem[8 + j, c] == u, c, 0)
             slot = jnp.minimum(slot, spheres - 1)
             for t in range(spheres):
                 last = meta_smem[2, t * slots + j * spheres + slot]
@@ -171,9 +193,10 @@
 
     def sweep_sum(sweep):
         scattered[...] = jnp.dot(operator[dev], coeffs[sweep, dev], preferred_element_type=f32)
-        for m in range(1, n_dev):
+        for m in others + [1] + [m + 1 for m in others]:
             peer = flipped(dev, m)
-            gather_copy(sweep, peer, dev).wait_recv()
+            if m % 2:
+                arrival(sweep, m).wait_recv()
             scattered[...] += jnp.dot(operator[peer], coeffs[sweep, peer], preferred_element_type=f32)
 
     def field_of(s):
@@ -211,32 +234,54 @@
             weighted[p, :, s * lanes : (s + 1) * lanes] = product.astype(jnp.bfloat16)
         return carry
 
-    lax.fori_loop(0, n_dev, weigh, 0)
+    early = n_dev * 5 // 8
+    lax.fori_loop(0, early, weigh, 0)
+    relay(1)
+    lax.fori_loop(early, n_dev, weigh, 0)
 
     sweep_sum(1)
     for s in range(spheres):
         final[s * rows : (s + 1) * rows, :] = apply_tmatrix(s, field_of(s))
 
-    def part_copy(source, target):
+    def part_copy(mask):
         return pltpu.make_async_remote_copy(
-            src_ref=part_send.at[target],
-            dst_ref=part_recv.at[source],
-            send_sem=send_sem.at[SWEEPS, target],
-            recv_sem=recv_sem.at[SWEEPS, source],
-            device_id=(grp, target),
+            src_ref=part_send.at[mask // 2],
+            dst_ref=part_recv.at[mask // 2],
+            send_sem=send_sem.at[SWEEPS, mask],
+            recv_sem=recv_sem.at[SWEEPS, mask],
+            device_id=(grp, flipped(dev, mask)),
             device_id_type=MESH,
         )
 
-    for m in range(1, n_dev):
-        peer = flipped(dev, m)
-        part = jnp.dot(weighted[peer], final[...], preferred_element_type=f32)
-        part_send[peer] = part.astype(part_send.dtype)
-        part_copy(dev, peer).start()
-    group_sum[...] = jnp.dot(weighted[dev], final[...], preferred_element_type=f32)
-    for m in range(1, n_dev):
-        peer = flipped(dev, m)
-        part_copy(peer, dev).wait_recv()
-        group_sum[...] += part_recv[peer].astype(f32)
+    def pair_copy(mask):
+        return pltpu.make_async_remote_copy(
+            src_ref=pair_send.at[mask // 2],
+            dst_ref=pair_recv.at[mask // 2],
+            send_sem=send_sem.at[SWEEPS, mask + 1],
+            recv_sem=recv_sem.at[SWEEPS, mask + 1],
+            device_id=(grp, sibling),
+            device_id_type=MESH,
+        )
+
+    def part(mask):
+        return jnp.dot(weighted[flipped(dev, mask)], final[...], preferred_element_type=f32)
+
+    far_order = others[::-1] + [0]
+    for m in far_order:
+        pair_send[m // 2] = part(m + 1)
+        pair_copy(m).start()
+    for m in far_order:
+        own = part(m)
+        pair_copy(m).wait_recv()
+        total = own + pair_recv[m // 2]
+        if m:
+            part_send[m // 2] = total.astype(part_send.dtype)
+            part_copy(m).start()
+        else:
+            group_sum[...] = total
+    for m in others:
+        part_copy(m).wait_recv()
+        group_sum[...] += part_recv[m // 2].astype(f32)
 
     def z_copy(source, target):
         return pltpu.make_async_remote_copy(
@@ -260,11 +305,15 @@
         out_ref[...] += z_recv[peer].astype(f32)
     for m in range(1, n_grp):
         z_copy(grp, (grp + m) % n_grp).wait_send()
-    for m in range(1, n_dev):
-        peer = flipped(dev, m)
-        for sweep in range(SWEEPS):
-            gather_copy(sweep, dev, peer).wait_send()
-        part_copy(dev, peer).wait_send()
+    for sweep in range(SWEEPS):
+        for m in others + [1]:
+            own_copy(sweep, m).wait_send()
+        for m in others:
+            relay_copy(sweep, m).wait_send()
+    for m in far_order:
+        pair_copy(m).wait_send()
+        if m:
+            part_copy(m).wait_send()
 
 
 def body(
@@ -291,7 +340,7 @@
     wide = spheres * rows
     bf16, f32 = jnp.bfloat16, jnp.float32
     z_type = bf16 if rows_out % 16 == 0 else f32
-    meta_shape = (8, max(pairs, spheres * n_dev * spheres))
+    meta_shape = (8 + (n_dev + 7) // 8 * 8, max(pairs, spheres * n_dev * spheres))
     smem = pl.BlockSpec(memory_space=pltpu.SMEM)
     vmem = pl.BlockSpec(memory_space=pltpu.VMEM)
     anywhere = pl.BlockSpec(memory_space=pl.ANY)
@@ -299,7 +348,7 @@
     return pl.pallas_call(
         functools.partial(kernel, n_grp, n_dev),
         out_shape=jax.ShapeDtypeStruct((rows_out, cols), f32),
-        in_specs=[smem] * 3 + [vmem] * 6 + [anywhere] * 2,
+        in_specs=[smem] * 2 + [vmem] * 7 + [anywhere] * 2,
         out_specs=vmem,
         scratch_shapes=[
             pltpu.VMEM(blocks.shape, bf16),
@@ -312,8 +361,10 @@
             pltpu.VMEM((chunk, 256), f32),
             pltpu.VMEM((n_dev, chunk, wide), bf16),
             pltpu.VMEM((wide, cols), f32),
-            pltpu.VMEM((n_dev, chunk, cols), bf16),
-            pltpu.VMEM((n_dev, chunk, cols), bf16),
+            pltpu.VMEM((n_dev // 2, chunk, cols), bf16),
+            pltpu.VMEM((n_dev // 2, chunk, cols), bf16),
+            pltpu.VMEM((n_dev // 2, chunk, cols), f32),
+            pltpu.VMEM((n_dev // 2, chunk, cols), f32),
             pltpu.VMEM((chunk, cols), f32),
             pltpu.VMEM((n_grp, rows_out, cols), z_type),
             pltpu.VMEM((n_grp, rows_out, cols), z_type),
@@ -333,8 +384,8 @@
         ),
     )(
         pair_count,
+        owner,
         need,
-        owner,
         pair_src,
         pair_tgt,
         pair_blk,

time: 50.4 us -> 45.8 us (0.909)
  Pallas kernels: 46.8 us -> 42.2 us
    pallas_call x1, Pallas kernels: 46.8 us -> 42.2 us  [body(): pl.pallas_call(functools.partial(kernel, n_grp, n_dev), out_shape=jax.Sha...]
where the time goes in v2:
time: 45.8 us; the launch traced here: 45.6 us
  Pallas kernels  42.2 us (92%)
  local copies, waits for them, and re-layouts  2.72 us (6%)
  between operations  0.66 us (1%)
    pallas_call x1, Pallas kernels, body(): pl.pallas_call(functools.partial(kernel, n_grp, n_dev), out_shape=jax.Sha...  42.2 us
    unnamed x2, local copies, waits for them, and re-layouts  2.72 us

profile of v2, /device:TPU:0, one launch (start us, length us, event | category | flops | bytes accessed | tf_op | source)
XLA Modules:
  0.0 45.6 jit_solution(3839038183222987746)
XLA Ops:
  0.7 1.3 %copy.12.need_ref = s32[1,8,4]{2,1,0:T(8,128)} copy(s32[1,8,4]{1,2,0:T(4,128)} %param.14) | data formatting | bytes 256 | tf_op args[3]
  2.0 42.2 %shard_map.109 = f32[64,128]{1,0:T(8,128)} custom-call(s32[1]{0:T(128)S(6)} %copy.14.count_ref, s32[2048]{0:T(1024)} %owner_ref.1, s32[1,8,4]{2,1,0:T(8,128)} %copy.12.need_ref, s32[1,512]{1,0:T(1,128)} %src_ref.1, s32[1,512]{1,0:T(1,128)} %tgt_ref.1, s32[1,512]{1,0:T(1,128)} %blk_ref.1, bf16[4,128,128]{2,1,0:T(8,128)(2,1)} %incident_ref.1, ...), custom_call_target="tpu_custom_call" | custom-call | tf_op jit(solution)/shard_map/pallas_call | solution.py:348
  44.2 1.4 %copy.15 = f32[64,128]{1,0:T(8,128)} copy(f32[64,128]{1,0:T(8,128)} %shard_map.109) | data formatting | bytes 65536

commit v3 on v2

--- a/solution.py
+++ b/solution.py
@@ -126,9 +126,6 @@
 
     for s in range(spheres):
         coeffs[0, dev, s * rows : (s + 1) * rows, :] = apply_tmatrix(s, incident_ref[s])
-    pl.semaphore_wait(barrier, n_dev - 1 + n_grp - 1)
-    send_coeffs(0)
-
     blk_bits, pair_bits = bits_for(n_blk), bits_for(pairs)
     place = lax.broadcasted_iota(jnp.int32, (1, pairs), 1)
     key = jnp.where(place < count_ref[0], tgt_ref[...] * slots + src_ref[...], cells)
@@ -154,14 +151,16 @@
         spot = lax.broadcasted_iota(jnp.int32, (1, lanes), 1) + k
         upto, under = count(key_col <= spot), count(key_col < spot)
         meta[2:3, k : k + lanes] = jnp.where(upto > under, upto - 1, pairs)
-    meta[8 : 8 + n_dev, 0:spheres] = need_ref[0]
+    meta[8 : 8 + spheres, 0:n_dev] = need_ref[0]
     to_smem = pltpu.make_async_copy(meta, meta_smem, load_sem.at[2])
     to_smem.start()
+    pl.semaphore_wait(barrier, n_dev - 1 + n_grp - 1)
+    send_coeffs(0)
     to_smem.wait()
     load_blocks.wait()
 
     sums[pairs] = jnp.zeros((rows, rows), jnp.bfloat16)
-    step = 4
+    step = 16
 
     def add_blocks(i, total):
         for k in range(step):
@@ -181,7 +180,7 @@
         for u in range(spheres):
             slot = 0
             for c in range(1, spheres):
-                slot = slot + jnp.where(meta_smem[8 + j, c] == u, c, 0)
+                slot = slot + jnp.where(meta_smem[8 + c, j] == u, c, 0)
             slot = jnp.minimum(slot, spheres - 1)
             for t in range(spheres):
                 last = meta_smem[2, t * slots + j * spheres + slot]
@@ -210,12 +209,12 @@
 
     load_harmonics.wait()
     factor_pad[...] = jnp.zeros_like(factor_pad)
+    factor_pad[0:spheres, :] = factor_ref[...]
     for k in range(0, n_dir, lanes):
-        factor_pad[0:spheres, :] = factor_ref[:, k : k + lanes]
-        table[k : k + lanes, lanes:] = jnp.transpose(factor_pad[...])
+        table[k : k + lanes, lanes:] = jnp.transpose(factor_pad[:, k : k + lanes])
         table[k : k + lanes, :lanes] = harmonics[k : k + lanes, :].astype(f32)
     chunk = n_grp * rows_out
-    row_step = 8
+    row_step = min(16, rows_out)
 
     def weigh(p, carry):
         for z in range(n_grp):
@@ -340,7 +339,7 @@
     wide = spheres * rows
     bf16, f32 = jnp.bfloat16, jnp.float32
     z_type = bf16 if rows_out % 16 == 0 else f32
-    meta_shape = (8 + (n_dev + 7) // 8 * 8, max(pairs, spheres * n_dev * spheres))
+    meta_shape = (8 + (spheres + 7) // 8 * 8, max(pairs, spheres * n_dev * spheres))
     smem = pl.BlockSpec(memory_space=pltpu.SMEM)
     vmem = pl.BlockSpec(memory_space=pltpu.VMEM)
     anywhere = pl.BlockSpec(memory_space=pl.ANY)
@@ -370,7 +369,7 @@
             pltpu.VMEM((n_grp, rows_out, cols), z_type),
             pltpu.VMEM((pairs, 128), jnp.int32),
             pltpu.VMEM((pairs, 128), jnp.int32),
-            pltpu.VMEM((128, 128), f32),
+            pltpu.VMEM((128, n_dir), f32),
             pltpu.VMEM(meta_shape, jnp.int32),
             pltpu.SMEM(meta_shape, jnp.int32),
             dma((3,)),
@@ -385,7 +384,7 @@
     )(
         pair_count,
         owner,
-        need,
+        need.transpose(0, 2, 1),
         pair_src,
         pair_tgt,
         pair_blk,

time: 45.8 us -> 44 us (0.961)
  local copies, waits for them, and re-layouts: 2.72 us -> 1.38 us
    unnamed x2 -> x1, local copies, waits for them, and re-layouts: 2.72 us -> 1.38 us
where the time goes in v3:
time: 44 us; the launch traced here: 43.8 us
  Pallas kernels  41.8 us (95%)
  local copies, waits for them, and re-layouts  1.38 us (3%)
  between operations  0.66 us (2%)
    pallas_call x1, Pallas kernels, body(): pl.pallas_call(functools.partial(kernel, n_grp, n_dev), out_shape=jax.Sha...  41.8 us
    unnamed x1, local copies, waits for them, and re-layouts  1.38 us

profile of v3, /device:TPU:0, one launch (start us, length us, event | category | flops | bytes accessed | tf_op | source)
XLA Modules:
  0.0 43.8 jit_solution(11109671910274742788)
XLA Ops:
  0.7 41.8 %shard_map.109 = f32[64,128]{1,0:T(8,128)} custom-call(s32[1]{0:T(128)S(6)} %copy.13.count_ref, s32[2048]{0:T(1024)} %owner_ref.1, s32[1,4,8]{2,1,0:T(4,128)} %bitcast.1, s32[1,512]{1,0:T(1,128)} %src_ref.1, s32[1,512]{1,0:T(1,128)} %tgt_ref.1, s32[1,512]{1,0:T(1,128)} %blk_ref.1, bf16[4,128,128]{2,1,0:T(8,128)(2,1)} %incident_ref.1, ...), custom_call_target="tpu_custom_call" | custom-call | tf_op jit(solution)/shard_map/pallas_call | solution.py:347
  42.4 1.4 %copy.14 = f32[64,128]{1,0:T(8,128)} copy(f32[64,128]{1,0:T(8,128)} %shard_map.109) | data formatting | bytes 65536

commit v4 on v3

--- a/solution.py
+++ b/solution.py
@@ -52,9 +52,8 @@
     scattered,
     part_send,
     part_recv,
-    pair_send,
+    far,
     pair_recv,
-    group_sum,
     z_send,
     z_recv,
     value_col,
@@ -65,6 +64,8 @@
     load_sem,
     send_sem,
     recv_sem,
+    part_send_sem,
+    part_recv_sem,
     z_send_sem,
     z_recv_sem,
 ):
@@ -124,8 +125,6 @@
     def apply_tmatrix(s, field):
         return jnp.dot(tmatrix_ref[s], field, preferred_element_type=f32).astype(jnp.bfloat16)
 
-    for s in range(spheres):
-        coeffs[0, dev, s * rows : (s + 1) * rows, :] = apply_tmatrix(s, incident_ref[s])
     blk_bits, pair_bits = bits_for(n_blk), bits_for(pairs)
     place = lax.broadcasted_iota(jnp.int32, (1, pairs), 1)
     key = jnp.where(place < count_ref[0], tgt_ref[...] * slots + src_ref[...], cells)
@@ -154,6 +153,8 @@
     meta[8 : 8 + spheres, 0:n_dev] = need_ref[0]
     to_smem = pltpu.make_async_copy(meta, meta_smem, load_sem.at[2])
     to_smem.start()
+    for s in range(spheres):
+        coeffs[0, dev, s * rows : (s + 1) * rows, :] = apply_tmatrix(s, incident_ref[s])
     pl.semaphore_wait(barrier, n_dev - 1 + n_grp - 1)
     send_coeffs(0)
     to_smem.wait()
@@ -213,106 +214,110 @@
     for k in range(0, n_dir, lanes):
         table[k : k + lanes, lanes:] = jnp.transpose(factor_pad[:, k : k + lanes])
         table[k : k + lanes, :lanes] = harmonics[k : k + lanes, :].astype(f32)
-    chunk = n_grp * rows_out
+    half = n_dev // 2
+    span = n_dev * rows_out
     row_step = min(16, rows_out)
 
-    def weigh(p, carry):
-        for z in range(n_grp):
-
-            def fetch(i, inner):
-                for k in range(row_step):
-                    row = i * row_step + k
-                    source = owner_ref[(z * n_dev + p) * rows_out + row]
-                    gathered[pl.ds(z * rows_out + row, 1), :] = table[pl.ds(source, 1), :]
-                return inner
-
-            lax.fori_loop(0, rows_out // row_step, fetch, 0)
+    def weigh(block, carry):
+        def fetch(i, inner):
+            first = block * lanes + i * row_step
+            place = (first % span) // rows_out
+            target = (place % half) * 2 + place // half
+            base = ((first // span) * n_dev + target) * rows_out + first % rows_out
+            for k in range(row_step):
+                source = owner_ref[base + k]
+                gathered[pl.ds(i * row_step + k, 1), :] = table[pl.ds(source, 1), :]
+            return inner
+
+        lax.fori_loop(0, lanes // row_step, fetch, 0)
+        there = pl.ds(pl.multiple_of(block * lanes, lanes), lanes)
         for s in range(spheres):
             phase = gathered[:, lanes + s : lanes + s + 1]
             product = phase * gathered[:, :lanes]
-            weighted[p, :, s * lanes : (s + 1) * lanes] = product.astype(jnp.bfloat16)
+            weighted[there, s * lanes : (s + 1) * lanes] = product.astype(jnp.bfloat16)
         return carry
 
-    early = n_dev * 5 // 8
+    early = n_dir // lanes * 5 // 8
     lax.fori_loop(0, early, weigh, 0)
     relay(1)
-    lax.fori_loop(early, n_dev, weigh, 0)
+    lax.fori_loop(early, n_dir // lanes, weigh, 0)
 
     sweep_sum(1)
     for s in range(spheres):
         final[s * rows : (s + 1) * rows, :] = apply_tmatrix(s, field_of(s))
 
-    def part_copy(mask):
+    core, chip = dev % 2, dev // 2
+
+    def pair_copy(turn):
         return pltpu.make_async_remote_copy(
-            src_ref=part_send.at[mask // 2],
-            dst_ref=part_recv.at[mask // 2],
-            send_sem=send_sem.at[SWEEPS, mask],
-            recv_sem=recv_sem.at[SWEEPS, mask],
+            src_ref=far.at[turn, 1 - core],
+            dst_ref=pair_recv.at[turn],
+            send_sem=part_send_sem.at[turn, 0],
+            recv_sem=part_recv_sem.at[turn, 0],
+            device_id=(grp, sibling),
+            device_id_type=MESH,
+        )
+
+    def part_copy(turn, mask):
+        return pltpu.make_async_remote_copy(
+            src_ref=part_send.at[turn, flipped(dev, mask) // 2],
+            dst_ref=part_recv.at[turn, mask // 2],
+            send_sem=part_send_sem.at[turn, mask // 2],
+            recv_sem=part_recv_sem.at[turn, mask // 2],
             device_id=(grp, flipped(dev, mask)),
             device_id_type=MESH,
         )
 
-    def pair_copy(mask):
+    def z_copy(turn):
         return pltpu.make_async_remote_copy(
-            src_ref=pair_send.at[mask // 2],
-            dst_ref=pair_recv.at[mask // 2],
-            send_sem=send_sem.at[SWEEPS, mask + 1],
-            recv_sem=recv_sem.at[SWEEPS, mask + 1],
-            device_id=(grp, sibling),
+            src_ref=z_send.at[turn],
+            dst_ref=z_recv.at[turn],
+            send_sem=z_send_sem.at[turn],
+            recv_sem=z_recv_sem.at[turn],
+            device_id=((grp + 1 + turn) % n_grp, dev),
             device_id_type=MESH,
         )
 
-    def part(mask):
-        return jnp.dot(weighted[flipped(dev, mask)], final[...], preferred_element_type=f32)
-
-    far_order = others[::-1] + [0]
-    for m in far_order:
-        pair_send[m // 2] = part(m + 1)
-        pair_copy(m).start()
-    for m in far_order:
-        own = part(m)
-        pair_copy(m).wait_recv()
-        total = own + pair_recv[m // 2]
-        if m:
-            part_send[m // 2] = total.astype(part_send.dtype)
-            part_copy(m).start()
+    for turn in range(n_grp):
+        z = (grp + 1 + turn) % n_grp
+        rows_of = pl.ds(pl.multiple_of(z * span, span), span)
+        result = jnp.dot(weighted[rows_of, :], final[...], preferred_element_type=f32)
+        for c in range(2):
+            far[turn, c] = result[c * half * rows_out : (c + 1) * half * rows_out, :]
+        pair_copy(turn).start()
+    for turn in range(n_grp):
+        pair_copy(turn).wait_recv()
+        total = far[turn, core] + pair_recv[turn]
+        for h in range(half):
+            piece = total[h * rows_out : (h + 1) * rows_out, :]
+            part_send[turn, h] = piece.astype(part_send.dtype)
+        for m in others[::-1]:
+            part_copy(turn, m).start()
+    for turn in range(n_grp):
+        mine = pl.ds(pl.multiple_of(chip * rows_out, rows_out), rows_out)
+        total = far[turn, core, mine, :] + pair_recv[turn, mine, :]
+        for m in others:
+            part_copy(turn, m).wait_recv()
+            total = total + part_recv[turn, m // 2].astype(f32)
+        if turn < n_grp - 1:
+            z_send[turn] = total.astype(z_send.dtype)
+            z_copy(turn).start()
         else:
-            group_sum[...] = total
-    for m in others:
-        part_copy(m).wait_recv()
-        group_sum[...] += part_recv[m // 2].astype(f32)
-
-    def z_copy(source, target):
-        return pltpu.make_async_remote_copy(
-            src_ref=z_send.at[target],
-            dst_ref=z_recv.at[source],
-            send_sem=z_send_sem.at[target],
-            recv_sem=z_recv_sem.at[source],
-            device_id=(target, dev),
-            device_id_type=MESH,
-        )
-
-    for z in range(n_grp):
-        z_send[z] = group_sum[z * rows_out : (z + 1) * rows_out, :].astype(z_send.dtype)
-    for m in range(1, n_grp):
-        z_copy(grp, (grp + m) % n_grp).start()
-    start = pl.multiple_of(grp * rows_out, rows_out)
-    out_ref[...] = group_sum[pl.ds(start, rows_out), :]
-    for m in range(1, n_grp):
-        peer = (grp + m) % n_grp
-        z_copy(peer, grp).wait_recv()
-        out_ref[...] += z_recv[peer].astype(f32)
-    for m in range(1, n_grp):
-        z_copy(grp, (grp + m) % n_grp).wait_send()
+            out_ref[...] = total
+    for turn in range(n_grp - 1):
+        z_copy(turn).wait_recv()
+        out_ref[...] += z_recv[turn].astype(f32)
+    for turn in range(n_grp):
+        pair_copy(turn).wait_send()
+        for m in others:
+            part_copy(turn, m).wait_send()
+        if turn < n_grp - 1:
+            z_copy(turn).wait_send()
     for sweep in range(SWEEPS):
         for m in others + [1]:
             own_copy(sweep, m).wait_send()
         for m in others:
             relay_copy(sweep, m).wait_send()
-    for m in far_order:
-        pair_copy(m).wait_send()
-        if m:
-            part_copy(m).wait_send()
 
 
 def body(
@@ -335,7 +340,7 @@
     pairs = pair_src.shape[1]
     n_dir = harmonics.shape[0]
     rows_out = n_dir // (n_grp * n_dev)
-    chunk = n_grp * rows_out
+    half = n_dev // 2
     wide = spheres * rows
     bf16, f32 = jnp.bfloat16, jnp.float32
     z_type = bf16 if rows_out % 16 == 0 else f32
@@ -357,14 +362,13 @@
             pltpu.VMEM((SWEEPS, n_dev, wide, cols), bf16),
             pltpu.VMEM((wide, cols), bf16),
             pltpu.VMEM((n_dir, 256), f32),
-            pltpu.VMEM((chunk, 256), f32),
-            pltpu.VMEM((n_dev, chunk, wide), bf16),
+            pltpu.VMEM((128, 256), f32),
+            pltpu.VMEM((n_dir, wide), bf16),
             pltpu.VMEM((wide, cols), f32),
-            pltpu.VMEM((n_dev // 2, chunk, cols), bf16),
-            pltpu.VMEM((n_dev // 2, chunk, cols), bf16),
-            pltpu.VMEM((n_dev // 2, chunk, cols), f32),
-            pltpu.VMEM((n_dev // 2, chunk, cols), f32),
-            pltpu.VMEM((chunk, cols), f32),
+            pltpu.VMEM((n_grp, half, rows_out, cols), z_type),
+            pltpu.VMEM((n_grp, half, rows_out, cols), z_type),
+            pltpu.VMEM((n_grp, 2, half * rows_out, cols), f32),
+            pltpu.VMEM((n_grp, half * rows_out, cols), f32),
             pltpu.VMEM((n_grp, rows_out, cols), z_type),
             pltpu.VMEM((n_grp, rows_out, cols), z_type),
             pltpu.VMEM((pairs, 128), jnp.int32),
@@ -373,8 +377,10 @@
             pltpu.VMEM(meta_shape, jnp.int32),
             pltpu.SMEM(meta_shape, jnp.int32),
             dma((3,)),
-            dma((SWEEPS + 1, n_dev)),
-            dma((SWEEPS + 1, n_dev)),
+            dma((SWEEPS, n_dev)),
+            dma((SWEEPS, n_dev)),
+            dma((n_grp, half)),
+            dma((n_grp, half)),
             dma((n_grp,)),
             dma((n_grp,)),
         ],

time: 44 us -> 44.1 us (level)
  no operation moved by 1% of the time
where the time goes in v4:
time: 44.1 us; the launch traced here: 43.9 us
  Pallas kernels  41.9 us (95%)
  local copies, waits for them, and re-layouts  1.38 us (3%)
  between operations  0.66 us (1%)
    pallas_call x1, Pallas kernels, body(): pl.pallas_call(functools.partial(kernel, n_grp, n_dev), out_shape=jax.Sha...  41.9 us
    unnamed x1, local copies, waits for them, and re-layouts  1.38 us

profile of v4, /device:TPU:0, one launch (start us, length us, event | category | flops | bytes accessed | tf_op | source)
XLA Modules:
  0.0 43.9 jit_solution(7404155477310003215)
XLA Ops:
  0.7 41.9 %shard_map.109 = f32[64,128]{1,0:T(8,128)} custom-call(s32[1]{0:T(128)S(6)} %copy.13.count_ref, s32[2048]{0:T(1024)} %owner_ref.1, s32[1,4,8]{2,1,0:T(4,128)} %bitcast.1, s32[1,512]{1,0:T(1,128)} %src_ref.1, s32[1,512]{1,0:T(1,128)} %tgt_ref.1, s32[1,512]{1,0:T(1,128)} %blk_ref.1, bf16[4,128,128]{2,1,0:T(8,128)(2,1)} %incident_ref.1, ...), custom_call_target="tpu_custom_call" | custom-call | tf_op jit(solution)/shard_map/pallas_call | solution.py:352
  42.5 1.4 %copy.14 = f32[64,128]{1,0:T(8,128)} copy(f32[64,128]{1,0:T(8,128)} %shard_map.109) | data formatting | bytes 65536

commit v5 on v4

--- a/solution.py
+++ b/solution.py
@@ -161,16 +161,21 @@
     load_blocks.wait()
 
     sums[pairs] = jnp.zeros((rows, rows), jnp.bfloat16)
-    step = 16
+    step = 4
 
     def add_blocks(i, total):
+        held, keeps = [], []
         for k in range(step):
             at = i * step + k
             before = jnp.maximum(at - 1, 0)
-            keep = jnp.where(meta_smem[1, at] == meta_smem[1, before], 1.0, 0.0)
-            block = jnp.clip(meta_smem[0, at], 0, n_blk - 1)
-            total = total * keep + blocks[block].astype(f32)
-            sums[at] = total.astype(jnp.bfloat16)
+            keeps.append(jnp.where(meta_smem[1, at] == meta_smem[1, before], 1.0, 0.0))
+            held.append(blocks[jnp.clip(meta_smem[0, at], 0, n_blk - 1)])
+        totals = []
+        for k in range(step):
+            total = total * keeps[k] + held[k].astype(f32)
+            totals.append(total.astype(jnp.bfloat16))
+        for k in range(step):
+            sums[i * step + k] = totals[k]
         return total
 
     lax.fori_loop(0, pairs // step, add_blocks, jnp.zeros((rows, rows), f32))
@@ -183,10 +188,12 @@
             for c in range(1, spheres):
                 slot = slot + jnp.where(meta_smem[8 + c, j] == u, c, 0)
             slot = jnp.minimum(slot, spheres - 1)
+            found = []
             for t in range(spheres):
                 last = meta_smem[2, t * slots + j * spheres + slot]
-                total = sums[jnp.clip(last, 0, pairs)]
-                operator[j, t * rows : (t + 1) * rows, u * rows : (u + 1) * rows] = total
+                found.append(sums[jnp.clip(last, 0, pairs)])
+            for t in range(spheres):
+                operator[j, t * rows : (t + 1) * rows, u * rows : (u + 1) * rows] = found[t]
         return carry
 
     lax.fori_loop(0, n_dev, place_cells, 0)
@@ -224,9 +231,9 @@
             place = (first % span) // rows_out
             target = (place % half) * 2 + place // half
             base = ((first // span) * n_dev + target) * rows_out + first % rows_out
+            found = [table[pl.ds(owner_ref[base + k], 1), :] for k in range(row_step)]
             for k in range(row_step):
-                source = owner_ref[base + k]
-                gathered[pl.ds(i * row_step + k, 1), :] = table[pl.ds(source, 1), :]
+                gathered[pl.ds(i * row_step + k, 1), :] = found[k]
             return inner
 
         lax.fori_loop(0, lanes // row_step, fetch, 0)

time: 44.1 us -> 44.1 us (level)
  no operation moved by 1% of the time
where the time goes in v5:
time: 44.1 us; the launch traced here: 43.9 us
  Pallas kernels  41.9 us (95%)
  local copies, waits for them, and re-layouts  1.38 us (3%)
  between operations  0.66 us (1%)
    pallas_call x1, Pallas kernels, body(): pl.pallas_call(functools.partial(kernel, n_grp, n_dev), out_shape=jax.Sha...  41.9 us
    unnamed x1, local copies, waits for them, and re-layouts  1.38 us

profile of v5, /device:TPU:0, one launch (start us, length us, event | category | flops | bytes accessed | tf_op | source)
XLA Modules:
  0.0 43.9 jit_solution(3018445556857548247)
XLA Ops:
  0.7 41.9 %shard_map.109 = f32[64,128]{1,0:T(8,128)} custom-call(s32[1]{0:T(128)S(6)} %copy.13.count_ref, s32[2048]{0:T(1024)} %owner_ref.1, s32[1,4,8]{2,1,0:T(4,128)} %bitcast.1, s32[1,512]{1,0:T(1,128)} %src_ref.1, s32[1,512]{1,0:T(1,128)} %tgt_ref.1, s32[1,512]{1,0:T(1,128)} %blk_ref.1, bf16[4,128,128]{2,1,0:T(8,128)(2,1)} %incident_ref.1, ...), custom_call_target="tpu_custom_call" | custom-call | tf_op jit(solution)/shard_map/pallas_call | solution.py:359
  42.5 1.4 %copy.14 = f32[64,128]{1,0:T(8,128)} copy(f32[64,128]{1,0:T(8,128)} %shard_map.109) | data formatting | bytes 65536
